TPU v7x, 32 devices: a whole 2x2x4 slice. The times are simulated.
32 devices in a mesh: grid: 8 (over y, x, core), band: 4 (over z).
Axes of the slice: x: 2, y: 2, z: 4, core: 2. Of those that a mesh axis runs over, the one named last changes fastest.
Arguments:
- orbitals: bfloat16 [8192, 512], P('grid', 'band'), may hold values from -6 to 6
- rotation: bfloat16 [512, 32768], P('grid', 'band'), may hold values from -0.25 to 0.25
Outputs:
- rotated: bfloat16 [8192, 32768], P('grid', 'band')
All inputs are finite; a program needn't handle non-finite values.
Results may differ from a plain program's by a relative error of at most 0.001.
Values may be sent and summed in bfloat16 or wider, within the bound.
A program may use at most 64 MiB of HBM per device.

v0:
```python
import jax
import jax.numpy as jnp
from jax import lax
from jax.sharding import PartitionSpec as P


def on_device(orbitals, rotation):
    all_cols = lax.all_gather(orbitals, "band", axis=1, tiled=True)
    all_rows = lax.all_gather(rotation, "grid", axis=0, tiled=True)
    total = jnp.dot(all_cols, all_rows, preferred_element_type=jnp.float32)
    return total.astype(jnp.bfloat16)


def solution(mesh):
    in_specs = (P("grid", "band"), P("grid", "band"))
    out_specs = P("grid", "band")
    return jax.shard_map(
        on_device, mesh=mesh, in_specs=in_specs, out_specs=out_specs, check_vma=False
    )
```

profile of v0, /device:TPU:0, one launch (start us, length us, event | category | flops | bytes accessed | tf_op | source)
XLA Modules:
  0.0 118.2 jit_solution(9894391133689167359)
XLA Ops:
  6.5 0.0 all-gather.3.cloned.1.call-start
  6.5 0.7 all-gather.3.cloned.1.call-update
  7.3 0.0 all-gather.5.cloned.1.call-start
  7.3 0.7 all-gather.5.cloned.1.call-update
  8.0 33.8 %all-gather.3.cloned.1.call-done = bf16[1024,512]{1,0:T(8,128)(2,1)} async-done(((bf16[1024,128]{1,0:T(8,128)(2,1)}), bf16[1024,512]{1,0:T(8,128)(2,1)}) %all-gather.3.cloned.1.call-update) | async-done | bytes 1048592 | tf_op jit(solution)/shard_map/all_gather | solution.py:8
  41.8 54.6 %all-gather.5.cloned.1.call-done = bf16[512,8192]{1,0:T(8,128)(2,1)} async-done(((bf16[64,8192]{1,0:T(8,128)(2,1)}), bf16[512,8192]{1,0:T(8,128)(2,1)}) %all-gather.5.cloned.1.call-update) | async-done | bytes 8388624 | tf_op jit(solution)/shard_map/all_gather | solution.py:9
  96.5 14.9 %convolution_convert_fusion = bf16[1024,8192]{1,0:T(8,128)(2,1)} fusion(bf16[1024,512]{1,0:T(8,128)(2,1)} %all-gather.3.cloned.1.call-done, bf16[512,8192]{1,0:T(8,128)(2,1)} %all-gather.5.cloned.1.call-done), kind=kOutput, calls=%fused_computation | convolution fusion | flops 8598323200 | bytes 26214400 | tf_op jit(solution)/shard_map/dot_general | solution.py:10
Async XLA Ops:
  6.5 35.3 %all-gather.3.cloned.1.call-start = ((), (), s32[]{:S(2)}) async-start(), calls=%async_computation | async-start | bytes 1310720 | tf_op jit(solution)/shard_map/all_gather | solution.py:8
  7.3 89.2 %all-gather.5.cloned.1.call-start = ((), (), s32[]{:S(2)}) async-start(), calls=%async_computation.1 | async-start | bytes 9437184 | tf_op jit(solution)/shard_map/all_gather | solution.py:9
Sparse Core Ops, SparseCore 0:
  8.9 32.8 all-gather.2
  43.7 52.6 all-gather.4
where the time goes:
time: 118 us
  waiting for transfers between devices  89.9 us (76%)
  matrix products  14.9 us (13%)
  between operations  13.4 us (11%)
    all_gather x1, waiting for transfers between devices, on_device(): all_rows = lax.all_gather(rotation, 'grid', axis=0, tiled=True)  54.6 us
    all_gather x1, waiting for transfers between devices, on_device(): all_cols = lax.all_gather(orbitals, 'band', axis=1, tiled=True)  33.8 us
    dot_general x1, matrix products, on_device(): total = jnp.dot(all_cols, all_rows, preferred_element_type=jnp.float32)  14.9 us
  transfers between devices with their start and end apart: 2, of which 2 were waited for; matrix products, arithmetic and copies ran while one was open for 0% of the time, Pallas kernels for 0%

commit v1 on v0

v1 whole, which is shorter than its diff:
```python
import functools

import jax
import jax.numpy as jnp
from jax import lax
from jax.experimental import pallas as pl
from jax.experimental.pallas import tpu as pltpu
from jax.sharding import PartitionSpec as P

CHUNKS = 16
EARLY = 4
AHEAD = 3


def gather_multiply(
    orb_ref, rot_ref, out_ref, gathered, points,
    early_send, early_recv, late_send, late_recv, pass_send, pass_recv,
    pair_send, pair_recv, line_send, line_recv, local_sem,
):
    depth, columns = rot_ref.shape
    inner = orb_ref.shape[1]
    half = depth // 2
    wide, narrow = columns // EARLY, columns // CHUNKS

    me = lax.axis_index("grid")
    z = lax.axis_index("band")
    nz = lax.axis_size("band")
    chip, core = me // 2, me % 2
    y, x = chip // 2, chip % 2
    chip_x = y * 2 + (1 - x)
    chip_y = (1 - y) * 2 + x
    chip_far = (1 - y) * 2 + (1 - x)
    sides = (chip_x, chip_y)

    def device(a_chip, a_core=core, a_z=z):
        return {"grid": a_chip * 2 + a_core, "band": a_z}

    first = (slice(0, half), slice(half, depth))

    def cols(j, width):
        return pl.ds(pl.multiple_of(j * width, width), width)

    def remote(src, dst, send, recv, to):
        return pltpu.make_async_remote_copy(
            src_ref=src, dst_ref=dst, send_sem=send, recv_sem=recv, device_id=to,
            device_id_type=pl.DeviceIdType.MESH,
        )

    def early(d, p):
        where = cols(p, wide)
        return remote(
            rot_ref.at[first[d], where], gathered.at[chip, core, first[d], where],
            early_send.at[d, p], early_recv.at[d, p], device(sides[d]))

    def late(d, j):
        where = cols(j, narrow)
        return remote(
            rot_ref.at[first[1 - d], where], gathered.at[chip, core, first[1 - d], where],
            late_send.at[d, j], late_recv.at[d, j], device(sides[d]))

    def passed(d, j):
        where = cols(j, narrow)
        ref = gathered.at[sides[1 - d], core, first[1 - d], where]
        return remote(ref, ref, pass_send.at[d, j], pass_recv.at[d, j], device(sides[d]))

    def pair(j):
        ref = gathered.at[:, core, :, cols(j, narrow)]
        return remote(ref, ref, pair_send.at[j], pair_recv.at[j], device(chip, 1 - core))

    def line(up, k):
        origin = z - k if up else z + k
        to = z + 1 if up else z - 1
        dst = points.at[:, pl.ds(pl.multiple_of(origin * inner, inner), inner)]
        d = 0 if up else 1
        return remote(
            orb_ref if k == 0 else dst, dst,
            line_send.at[d, k], line_recv.at[d, k], device(chip, core, to))

    def line_has(up, k):
        return (z >= k) & (z < nz - 1) if up else (z <= nz - 1 - k) & (z > 0)

    def line_gets(up, k):
        return z >= k + 1 if up else z <= nz - 2 - k

    def line_step(k):
        for up in (True, False):
            if k > 0:
                @pl.when(line_gets(up, k - 1))
                def _():
                    line(up, k - 1).wait_recv()
            if k < 3:
                @pl.when(line_has(up, k))
                def _():
                    line(up, k).start()

    barrier = pltpu.get_barrier_semaphore()

    def greet(to):
        pl.semaphore_signal(barrier, inc=1, device_id=to, device_id_type=pl.DeviceIdType.MESH)

    own_rot = pltpu.make_async_copy(rot_ref, gathered.at[chip, core], local_sem.at[0])
    own_orb = pltpu.make_async_copy(
        orb_ref, points.at[:, pl.ds(pl.multiple_of(z * inner, inner), inner)], local_sem.at[1])
    own_rot.start()
    own_orb.start()

    for to in (device(chip_x), device(chip_y), device(chip, 1 - core)):
        greet(to)

    @pl.when(z > 0)
    def _():
        greet(device(chip, core, z - 1))

    @pl.when(z < nz - 1)
    def _():
        greet(device(chip, core, z + 1))

    middle = (z > 0) & (z < nz - 1)

    @pl.when(middle)
    def _():
        pl.semaphore_wait(barrier, 5)

    @pl.when(jnp.logical_not(middle))
    def _():
        pl.semaphore_wait(barrier, 4)

    def start_early(p):
        for d in (0, 1):
            early(d, p).start()

    def got_early(p):
        for d in (0, 1):
            early(d, p).wait_recv()

    def start_late(j):
        for d in (0, 1):
            late(d, j).start()
            passed(d, j).start()

    def exchange(j):
        for d in (0, 1):
            late(d, j).wait_recv()
            passed(d, j).wait_recv()
        pair(j).start()

    def multiply(j):
        pair(j).wait_recv()
        where = cols(j, narrow)
        block = gathered[:, :, :, where].reshape(8 * depth, narrow)
        out_ref[:, where] = jnp.dot(
            points[...], block, preferred_element_type=jnp.float32
        ).astype(out_ref.dtype)

    line_step(0)
    start_early(0)
    start_early(1)
    got_early(0)
    start_early(2)
    got_early(1)
    line_step(1)
    start_early(3)
    own_rot.wait()
    own_orb.wait()
    got_early(2)
    start_late(0)
    start_late(1)
    got_early(3)
    line_step(2)
    start_late(2)

    def receive(j, _):
        exchange(j)
        start_late(j + AHEAD)
        return 0

    lax.fori_loop(0, 4, receive, 0)
    line_step(3)

    def catch_up(j, _):
        receive(j, 0)

        def one(i, _):
            multiply(i)
            return 0

        lax.fori_loop(2 * (j - 4), 2 * (j - 4) + 2, one, 0)
        return 0

    lax.fori_loop(4, 8, catch_up, 0)

    def steady(j, _):
        exchange(j)

        @pl.when(j + AHEAD < CHUNKS)
        def _():
            start_late(j + AHEAD)

        multiply(j - 1)
        return 0

    exchange(8)
    start_late(8 + AHEAD)
    lax.fori_loop(9, CHUNKS, steady, 0)
    multiply(CHUNKS - 1)

    for p in range(EARLY):
        for d in (0, 1):
            early(d, p).wait_send()

    def sent(j, _):
        for d in (0, 1):
            late(d, j).wait_send()
            passed(d, j).wait_send()
        pair(j).wait_send()
        return 0

    lax.fori_loop(0, CHUNKS, sent, 0)
    for k in range(3):
        for up in (True, False):
            @pl.when(line_has(up, k))
            def _():
                line(up, k).wait_send()


def in_kernel(orbitals, rotation):
    points, inner = orbitals.shape
    depth, columns = rotation.shape
    dma = pltpu.SemaphoreType.DMA
    return pl.pallas_call(
        gather_multiply,
        out_shape=pltpu.VMEM((points, columns), jnp.bfloat16),
        in_specs=[pl.BlockSpec(memory_space=pl.ANY)] * 2,
        out_specs=pl.BlockSpec(memory_space=pltpu.VMEM),
        scratch_shapes=[
            pltpu.VMEM((4, 2, depth, columns), jnp.bfloat16),
            pltpu.VMEM((points, 4 * inner), jnp.bfloat16),
            dma((2, EARLY)), dma((2, EARLY)),
            dma((2, CHUNKS)), dma((2, CHUNKS)),
            dma((2, CHUNKS)), dma((2, CHUNKS)),
            dma((CHUNKS,)), dma((CHUNKS,)),
            dma((2, 3)), dma((2, 3)),
            dma((2,)),
        ],
        compiler_params=pltpu.CompilerParams(
            collective_id=0, has_side_effects=True, vmem_limit_bytes=20 * 2**20
        ),
        cost_estimate=pl.CostEstimate(
            flops=2 * points * 8 * depth * columns,
            bytes_accessed=2 * (points * columns + points * inner + depth * columns),
            transcendentals=0,
        ),
        name="gather_multiply",
    )(orbitals, rotation)


def with_collectives(orbitals, rotation):
    all_cols = lax.all_gather(orbitals, "band", axis=1, tiled=True)
    all_rows = lax.all_gather(rotation, "grid", axis=0, tiled=True)
    total = jnp.dot(all_cols, all_rows, preferred_element_type=jnp.float32)
    return total.astype(jnp.bfloat16)


def solution(mesh):
    specs = (P("grid", "band"), P("grid", "band"))

    def on_device(orbitals, rotation):
        square = mesh.shape["grid"] == 8 and mesh.shape["band"] == 4
        fits = (
            orbitals.shape[1] % 128 == 0
            and rotation.shape[0] % 64 == 0
            and rotation.shape[1] % (128 * CHUNKS) == 0
        )
        return (in_kernel if square and fits else with_collectives)(orbitals, rotation)

    return jax.shard_map(
        on_device, mesh=mesh, in_specs=specs, out_specs=P("grid", "band"), check_vma=False
    )
```

time: 118 us -> 53.2 us (0.45)
  waiting for transfers between devices: 89.9 us -> 0 us
  Pallas kernels: 0 us -> 44.7 us
  matrix products: 14.9 us -> 0 us
  between operations: 13.4 us -> 0.01 us
  local copies, waits for them, and re-layouts: 0 us -> 8.34 us
    all_gather x2 -> x0, waiting for transfers between devices: 88.5 us -> none  [the longest x1 54.6 us: on_device(): all_rows = lax.all_gather(rotation, 'grid', axis=0, tiled=True)]
    pallas_call x0 -> x1, Pallas kernels: none -> 44.7 us  [in_kernel(): pl.pallas_call(gather_multiply, out_shape=pltpu.VMEM((points, columns), j...]
    dot_general x1 -> x0, matrix products: 14.9 us -> none  [on_device(): total = jnp.dot(all_cols, all_rows, preferred_element_type=jnp.float32)]
    unnamed x0 -> x5, local copies, waits for them, and re-layouts: none -> 8.34 us
    unnamed x2 -> x0, waiting for transfers between devices: 1.41 us -> none
  transfers between devices with their start and end apart: 2 -> 0, of which waited for: 2 -> 0; matrix products, arithmetic and copies ran while one was open for 0% -> 0% of each run, Pallas kernels for 0% -> 0%
where the time goes in v1:
time: 53.2 us; the launch traced here: 53 us
  Pallas kernels  44.7 us (84%)
  local copies, waits for them, and re-layouts  8.34 us (16%)
    pallas_call x1, Pallas kernels, in_kernel(): pl.pallas_call(gather_multiply, out_shape=pltpu.VMEM((points, columns), j...  44.7 us
    unnamed x5, local copies, waits for them, and re-layouts  8.34 us

profile of v1, /device:TPU:0, one launch (start us, length us, event | category | flops | bytes accessed | tf_op | source)
XLA Modules:
  0.0 53.0 jit_solution(1355270764591708707)
XLA Ops:
  0.0 0.0 copy-start
  0.0 1.2 %copy-done = bf16[64,8192]{1,0:T(8,128)(2,1)S(1)} copy-done((bf16[64,8192]{1,0:T(8,128)(2,1)S(1)}, bf16[64,8192]{1,0:T(8,128)(2,1)}, u32[]{:S(2)}) %copy-start) | copy-done | bytes 1048600
  1.2 0.0 copy-start.1
  1.2 0.9 %copy-done.1 = bf16[1024,128]{1,0:T(8,128)(2,1)S(1)} copy-done((bf16[1024,128]{1,0:T(8,128)(2,1)S(1)}, bf16[1024,128]{1,0:T(8,128)(2,1)}, u32[]{:S(2)}) %copy-start.1) | copy-done | bytes 262168
  2.2 44.7 %gather_multiply.1 = bf16[1024,8192]{1,0:T(8,128)(2,1)S(1)} custom-call(bf16[1024,128]{1,0:T(8,128)(2,1)S(1)} %copy-done.1, bf16[64,8192]{1,0:T(8,128)(2,1)S(1)} %copy-done), custom_call_target="tpu_custom_call" | custom-call | flops 8589934592 | bytes 18087936 | tf_op jit(solution)/shard_map/gather_multiply/pallas_call | solution.py:230
  46.8 6.2 %copy.4 = bf16[1024,8192]{1,0:T(8,128)(2,1)} copy(bf16[1024,8192]{1,0:T(8,128)(2,1)S(1)} %gather_multiply.1) | data formatting | bytes 33554432
Async XLA Ops:
  0.0 1.2 %copy-start = (bf16[64,8192]{1,0:T(8,128)(2,1)S(1)}, bf16[64,8192]{1,0:T(8,128)(2,1)}, u32[]{:S(2)}) copy-start(bf16[64,8192]{1,0:T(8,128)(2,1)} %rot_ref.1) | copy-start | bytes 3145732
  1.2 0.9 %copy-start.1 = (bf16[1024,128]{1,0:T(8,128)(2,1)S(1)}, bf16[1024,128]{1,0:T(8,128)(2,1)}, u32[]{:S(2)}) copy-start(bf16[1024,128]{1,0:T(8,128)(2,1)} %orb_ref.1) | copy-start | bytes 786436

commit v2 on v1

--- a/solution.py
+++ b/solution.py
@@ -9,12 +9,13 @@
 
 CHUNKS = 16
 EARLY = 4
-AHEAD = 3
+AHEAD = 5
+LEFT = 4
 
 
 def gather_multiply(
     orb_ref, rot_ref, out_ref, gathered, points,
-    early_send, early_recv, late_send, late_recv, pass_send, pass_recv,
+    early_send, early_recv, late_send, late_recv,
     pair_send, pair_recv, line_send, line_recv, local_sem,
 ):
     depth, columns = rot_ref.shape
@@ -49,22 +50,19 @@
     def early(d, p):
         where = cols(p, wide)
         return remote(
-            rot_ref.at[first[d], where], gathered.at[chip, core, first[d], where],
+            rot_ref.at[first[d], where], gathered.at[y, x, core, first[d], where],
             early_send.at[d, p], early_recv.at[d, p], device(sides[d]))
 
     def late(d, j):
         where = cols(j, narrow)
-        return remote(
-            rot_ref.at[first[1 - d], where], gathered.at[chip, core, first[1 - d], where],
-            late_send.at[d, j], late_recv.at[d, j], device(sides[d]))
-
-    def passed(d, j):
-        where = cols(j, narrow)
-        ref = gathered.at[sides[1 - d], core, first[1 - d], where]
-        return remote(ref, ref, pass_send.at[d, j], pass_recv.at[d, j], device(sides[d]))
+        if d == 0:
+            ref = gathered.at[:, x, core, first[1], where]
+        else:
+            ref = gathered.at[y, :, core, first[0], where]
+        return remote(ref, ref, late_send.at[d, j], late_recv.at[d, j], device(sides[d]))
 
     def pair(j):
-        ref = gathered.at[:, core, :, cols(j, narrow)]
+        ref = gathered.at[:, :, core, :, cols(j, narrow)]
         return remote(ref, ref, pair_send.at[j], pair_recv.at[j], device(chip, 1 - core))
 
     def line(up, k):
@@ -98,7 +96,7 @@
     def greet(to):
         pl.semaphore_signal(barrier, inc=1, device_id=to, device_id_type=pl.DeviceIdType.MESH)
 
-    own_rot = pltpu.make_async_copy(rot_ref, gathered.at[chip, core], local_sem.at[0])
+    own_rot = pltpu.make_async_copy(rot_ref, gathered.at[y, x, core], local_sem.at[0])
     own_orb = pltpu.make_async_copy(
         orb_ref, points.at[:, pl.ds(pl.multiple_of(z * inner, inner), inner)], local_sem.at[1])
     own_rot.start()
@@ -136,18 +134,16 @@
     def start_late(j):
         for d in (0, 1):
             late(d, j).start()
-            passed(d, j).start()
 
     def exchange(j):
         for d in (0, 1):
             late(d, j).wait_recv()
-            passed(d, j).wait_recv()
         pair(j).start()
 
     def multiply(j):
         pair(j).wait_recv()
         where = cols(j, narrow)
-        block = gathered[:, :, :, where].reshape(8 * depth, narrow)
+        block = gathered[:, :, :, :, where].reshape(8 * depth, narrow)
         out_ref[:, where] = jnp.dot(
             points[...], block, preferred_element_type=jnp.float32
         ).astype(out_ref.dtype)
@@ -155,23 +151,28 @@
     line_step(0)
     start_early(0)
     start_early(1)
+    own_rot.wait()
+    own_orb.wait()
     got_early(0)
     start_early(2)
     got_early(1)
+    start_early(3)
     line_step(1)
-    start_early(3)
-    own_rot.wait()
-    own_orb.wait()
     got_early(2)
-    start_late(0)
-    start_late(1)
+    for j in range(3):
+        start_late(j)
     got_early(3)
+    for j in range(3, AHEAD):
+        start_late(j)
     line_step(2)
-    start_late(2)
 
     def receive(j, _):
         exchange(j)
-        start_late(j + AHEAD)
+
+        @pl.when(j + AHEAD < CHUNKS)
+        def _():
+            start_late(j + AHEAD)
+
         return 0
 
     lax.fori_loop(0, 4, receive, 0)
@@ -188,21 +189,26 @@
         return 0
 
     lax.fori_loop(4, 8, catch_up, 0)
+    receive(8, 0)
 
     def steady(j, _):
-        exchange(j)
-
-        @pl.when(j + AHEAD < CHUNKS)
-        def _():
-            start_late(j + AHEAD)
-
+        receive(j, 0)
         multiply(j - 1)
         return 0
 
-    exchange(8)
-    start_late(8 + AHEAD)
-    lax.fori_loop(9, CHUNKS, steady, 0)
-    multiply(CHUNKS - 1)
+    lax.fori_loop(9, CHUNKS - LEFT + 1, steady, 0)
+
+    def last(j, _):
+        receive(j, 0)
+        return 0
+
+    lax.fori_loop(CHUNKS - LEFT + 1, CHUNKS, last, 0)
+
+    def arrived(j, _):
+        pair(j).wait_recv()
+        return 0
+
+    lax.fori_loop(CHUNKS - LEFT, CHUNKS, arrived, 0)
 
     for p in range(EARLY):
         for d in (0, 1):
@@ -211,7 +217,6 @@
     def sent(j, _):
         for d in (0, 1):
             late(d, j).wait_send()
-            passed(d, j).wait_send()
         pair(j).wait_send()
         return 0
 
@@ -223,35 +228,95 @@
                 line(up, k).wait_send()
 
 
+def write_rest(first_ref, gathered, points, out_ref, last, sems):
+    rows, done = first_ref.shape
+    columns = out_ref.shape[1]
+    narrow = (columns - done) // LEFT
+    depth = points.shape[1]
+    block = rows // LEFT
+    copies = []
+    for i in range(LEFT):
+        part = pl.ds(i * block, block)
+        copies.append(pltpu.make_async_copy(
+            first_ref.at[part], out_ref.at[part, pl.ds(0, done)], sems.at[i]))
+        copies[-1].start()
+
+    def put(i):
+        start = pl.multiple_of(i * narrow, narrow)
+        at = pl.multiple_of(done + i * narrow, narrow)
+        return pltpu.make_async_copy(
+            last.at[:, pl.ds(start, narrow)], out_ref.at[:, pl.ds(at, narrow)],
+            sems.at[LEFT + i])
+
+    def multiply(i, _):
+        at = pl.ds(pl.multiple_of(done + i * narrow, narrow), narrow)
+        where = pl.ds(pl.multiple_of(i * narrow, narrow), narrow)
+        weights = gathered[:, :, :, :, at].reshape(depth, narrow)
+        last[:, where] = jnp.dot(
+            points[...], weights, preferred_element_type=jnp.float32
+        ).astype(last.dtype)
+        put(i).start()
+        return 0
+
+    lax.fori_loop(0, LEFT, multiply, 0)
+    for copy in copies:
+        copy.wait()
+    for i in range(LEFT):
+        put(i).wait()
+
+
 def in_kernel(orbitals, rotation):
     points, inner = orbitals.shape
     depth, columns = rotation.shape
+    bf16 = jnp.bfloat16
+    rest = columns // CHUNKS * LEFT
     dma = pltpu.SemaphoreType.DMA
-    return pl.pallas_call(
+    vmem = pl.BlockSpec(memory_space=pltpu.VMEM)
+    hbm = pl.BlockSpec(memory_space=pltpu.HBM)
+    first, gathered, all_points = pl.pallas_call(
         gather_multiply,
-        out_shape=pltpu.VMEM((points, columns), jnp.bfloat16),
-        in_specs=[pl.BlockSpec(memory_space=pl.ANY)] * 2,
-        out_specs=pl.BlockSpec(memory_space=pltpu.VMEM),
+        out_shape=(
+            pltpu.VMEM((points, columns - rest), bf16),
+            pltpu.VMEM((2, 2, 2, depth, columns), bf16),
+            pltpu.VMEM((points, 4 * inner), bf16),
+        ),
+        in_specs=[hbm] * 2,
+        out_specs=(vmem,) * 3,
         scratch_shapes=[
-            pltpu.VMEM((4, 2, depth, columns), jnp.bfloat16),
-            pltpu.VMEM((points, 4 * inner), jnp.bfloat16),
             dma((2, EARLY)), dma((2, EARLY)),
-            dma((2, CHUNKS)), dma((2, CHUNKS)),
             dma((2, CHUNKS)), dma((2, CHUNKS)),
             dma((CHUNKS,)), dma((CHUNKS,)),
             dma((2, 3)), dma((2, 3)),
             dma((2,)),
         ],
         compiler_params=pltpu.CompilerParams(
-            collective_id=0, has_side_effects=True, vmem_limit_bytes=20 * 2**20
+            collective_id=0, has_side_effects=True, vmem_limit_bytes=16 * 2**20
         ),
         cost_estimate=pl.CostEstimate(
-            flops=2 * points * 8 * depth * columns,
-            bytes_accessed=2 * (points * columns + points * inner + depth * columns),
+            flops=2 * points * 8 * depth * (columns - rest),
+            bytes_accessed=2 * (points * inner + depth * columns),
             transcendentals=0,
         ),
         name="gather_multiply",
-    )(orbitals, rotation)
+    )(
+        pltpu.with_memory_space_constraint(orbitals, pltpu.HBM),
+        pltpu.with_memory_space_constraint(rotation, pltpu.HBM),
+    )
+    keep = functools.partial(pltpu.with_memory_space_constraint, memory_space=pltpu.VMEM)
+    return pl.pallas_call(
+        write_rest,
+        out_shape=pltpu.HBM((points, columns), bf16),
+        in_specs=[vmem] * 3,
+        out_specs=hbm,
+        scratch_shapes=[pltpu.VMEM((points, rest), bf16), dma((2 * LEFT,))],
+        compiler_params=pltpu.CompilerParams(vmem_limit_bytes=16 * 2**20),
+        cost_estimate=pl.CostEstimate(
+            flops=2 * points * 8 * depth * rest,
+            bytes_accessed=2 * points * columns,
+            transcendentals=0,
+        ),
+        name="write_rest",
+    )(keep(first), keep(gathered), keep(all_points))
 
 
 def with_collectives(orbitals, rotation):

time: 53.2 us -> 47.4 us (0.89)
  local copies, waits for them, and re-layouts: 8.34 us -> 0 us
  Pallas kernels: 44.7 us -> 47.2 us
    unnamed x5 -> x0, local copies, waits for them, and re-layouts: 8.34 us -> none
    pallas_call x1 -> x2, Pallas kernels: 44.7 us -> 47.2 us  [the longest x1 41.3 us: in_kernel(): pl.pallas_call(gather_multiply, out_shape=(pltpu.VMEM((points, columns -...]
where the time goes in v2:
time: 47.4 us; the launch traced here: 47.2 us
  Pallas kernels  47.2 us (100%)
    pallas_call x1, Pallas kernels, in_kernel(): pl.pallas_call(gather_multiply, out_shape=(pltpu.VMEM((points, columns -...  41.3 us
    pallas_call x1, Pallas kernels, in_kernel(): pl.pallas_call(write_rest, out_shape=pltpu.HBM((points, columns), bf16),...  5.95 us

profile of v2, /device:TPU:0, one launch (start us, length us, event | category | flops | bytes accessed | tf_op | source)
XLA Modules:
  0.0 47.2 jit_solution(10646343681276849185)
XLA Ops:
  0.0 41.3 %gather_multiply.1 = (bf16[1024,6144]{1,0:T(8,128)(2,1)S(1)}, bf16[2,2,2,64,8192]{4,3,2,1,0:T(8,128)(2,1)S(1)}, bf16[1024,512]{1,0:T(8,128)(2,1)S(1)}) custom-call(bf16[1024,128]{1,0:T(8,128)(2,1)} %orb_ref.1, bf16[64,8192]{1,0:T(8,128)(2,1)} %rot_ref.1), custom_call_target="tpu_custom_call" | custom-call | flops 6442450944 | bytes 1310720 | tf_op jit(solution)/shard_map/gather_multiply/pallas_call | solution.py:276
  41.3 6.0 %write_rest.1 = bf16[1024,8192]{1,0:T(8,128)(2,1)} custom-call(bf16[1024,6144]{1,0:T(8,128)(2,1)S(1)} %get-tuple-element.8.first_ref, bf16[2,2,2,64,8192]{4,3,2,1,0:T(8,128)(2,1)S(1)} %get-tuple-element.9.gathered, bf16[1024,512]{1,0:T(8,128)(2,1)S(1)} %get-tuple-element.10.points), custom_call_target="tpu_custom_call" | custom-call | flops 2147483648 | bytes 16777216 | tf_op jit(solution)/shard_map/write_rest/pallas_call | solution.py:306

commit v3 on v2

--- a/solution.py
+++ b/solution.py
@@ -9,8 +9,9 @@
 
 CHUNKS = 16
 EARLY = 4
-AHEAD = 5
-LEFT = 4
+AHEAD = 8
+LEFT = 2
+BLOCKS = 8
 
 
 def gather_multiply(
@@ -149,20 +150,21 @@
         ).astype(out_ref.dtype)
 
     line_step(0)
-    start_early(0)
-    start_early(1)
+    for p in range(3):
+        start_early(p)
     own_rot.wait()
     own_orb.wait()
     got_early(0)
-    start_early(2)
+    start_early(3)
     got_early(1)
-    start_early(3)
+    for j in range(2):
+        start_late(j)
     line_step(1)
     got_early(2)
-    for j in range(3):
+    for j in range(2, 5):
         start_late(j)
     got_early(3)
-    for j in range(3, AHEAD):
+    for j in range(5, AHEAD):
         start_late(j)
     line_step(2)
 
@@ -233,9 +235,9 @@
     columns = out_ref.shape[1]
     narrow = (columns - done) // LEFT
     depth = points.shape[1]
-    block = rows // LEFT
+    block = rows // BLOCKS
     copies = []
-    for i in range(LEFT):
+    for i in range(BLOCKS):
         part = pl.ds(i * block, block)
         copies.append(pltpu.make_async_copy(
             first_ref.at[part], out_ref.at[part, pl.ds(0, done)], sems.at[i]))
@@ -246,7 +248,7 @@
         at = pl.multiple_of(done + i * narrow, narrow)
         return pltpu.make_async_copy(
             last.at[:, pl.ds(start, narrow)], out_ref.at[:, pl.ds(at, narrow)],
-            sems.at[LEFT + i])
+            sems.at[BLOCKS + i])
 
     def multiply(i, _):
         at = pl.ds(pl.multiple_of(done + i * narrow, narrow), narrow)
@@ -308,7 +310,7 @@
         out_shape=pltpu.HBM((points, columns), bf16),
         in_specs=[vmem] * 3,
         out_specs=hbm,
-        scratch_shapes=[pltpu.VMEM((points, rest), bf16), dma((2 * LEFT,))],
+        scratch_shapes=[pltpu.VMEM((points, rest), bf16), dma((BLOCKS + LEFT,))],
         compiler_params=pltpu.CompilerParams(vmem_limit_bytes=16 * 2**20),
         cost_estimate=pl.CostEstimate(
             flops=2 * points * 8 * depth * rest,

time: 47.4 us -> 47.8 us (level)
  Pallas kernels: 47.2 us -> 47.7 us
    pallas_call x1, Pallas kernels: 41.3 us -> 41.7 us  [in_kernel(): pl.pallas_call(gather_multiply, out_shape=(pltpu.VMEM((points, columns -...]
where the time goes in v3:
time: 47.8 us; the launch traced here: 47.7 us
  Pallas kernels  47.7 us (100%)
    pallas_call x1, Pallas kernels, in_kernel(): pl.pallas_call(gather_multiply, out_shape=(pltpu.VMEM((points, columns -...  41.7 us
    pallas_call x1, Pallas kernels, in_kernel(): pl.pallas_call(write_rest, out_shape=pltpu.HBM((points, columns), bf16),...  5.95 us

profile of v3, /device:TPU:0, one launch (start us, length us, event | category | flops | bytes accessed | tf_op | source)
XLA Modules:
  0.0 47.7 jit_solution(6313693728014568752)
XLA Ops:
  0.0 41.7 %gather_multiply.1 = (bf16[1024,7168]{1,0:T(8,128)(2,1)S(1)}, bf16[2,2,2,64,8192]{4,3,2,1,0:T(8,128)(2,1)S(1)}, bf16[1024,512]{1,0:T(8,128)(2,1)S(1)}) custom-call(bf16[1024,128]{1,0:T(8,128)(2,1)} %orb_ref.1, bf16[64,8192]{1,0:T(8,128)(2,1)} %rot_ref.1), custom_call_target="tpu_custom_call" | custom-call | flops 7516192768 | bytes 1310720 | tf_op jit(solution)/shard_map/gather_multiply/pallas_call | solution.py:278
  41.8 5.9 %write_rest.1 = bf16[1024,8192]{1,0:T(8,128)(2,1)} custom-call(bf16[1024,7168]{1,0:T(8,128)(2,1)S(1)} %get-tuple-element.8.first_ref, bf16[2,2,2,64,8192]{4,3,2,1,0:T(8,128)(2,1)S(1)} %get-tuple-element.9.gathered, bf16[1024,512]{1,0:T(8,128)(2,1)S(1)} %get-tuple-element.10.points), custom_call_target="tpu_custom_call" | custom-call | flops 1073741824 | bytes 16777216 | tf_op jit(solution)/shard_map/write_rest/pallas_call | solution.py:308

commit v4 on v2

--- a/solution.py
+++ b/solution.py
@@ -8,20 +8,21 @@
 from jax.sharding import PartitionSpec as P
 
 CHUNKS = 16
-EARLY = 4
+GROUP = 4
 AHEAD = 5
 LEFT = 4
+BLOCKS = 8
 
 
 def gather_multiply(
     orb_ref, rot_ref, out_ref, gathered, points,
     early_send, early_recv, late_send, late_recv,
-    pair_send, pair_recv, line_send, line_recv, local_sem,
+    pair_send, pair_recv, line_send, line_recv, own_sem, local_sem,
 ):
     depth, columns = rot_ref.shape
     inner = orb_ref.shape[1]
     half = depth // 2
-    wide, narrow = columns // EARLY, columns // CHUNKS
+    narrow = columns // CHUNKS
 
     me = lax.axis_index("grid")
     z = lax.axis_index("band")
@@ -48,21 +49,20 @@
         )
 
     def early(d, p):
-        where = cols(p, wide)
+        where = cols(p, narrow)
         return remote(
-            rot_ref.at[first[d], where], gathered.at[y, x, core, first[d], where],
+            rot_ref.at[first[d], where], gathered.at[p, y, x, core, first[d]],
             early_send.at[d, p], early_recv.at[d, p], device(sides[d]))
 
     def late(d, j):
-        where = cols(j, narrow)
         if d == 0:
-            ref = gathered.at[:, x, core, first[1], where]
+            ref = gathered.at[j, :, x, core, first[1]]
         else:
-            ref = gathered.at[y, :, core, first[0], where]
+            ref = gathered.at[j, y, :, core, first[0]]
         return remote(ref, ref, late_send.at[d, j], late_recv.at[d, j], device(sides[d]))
 
     def pair(j):
-        ref = gathered.at[:, :, core, :, cols(j, narrow)]
+        ref = gathered.at[j, :, :, core]
         return remote(ref, ref, pair_send.at[j], pair_recv.at[j], device(chip, 1 - core))
 
     def line(up, k):
@@ -96,10 +96,20 @@
     def greet(to):
         pl.semaphore_signal(barrier, inc=1, device_id=to, device_id_type=pl.DeviceIdType.MESH)
 
-    own_rot = pltpu.make_async_copy(rot_ref, gathered.at[y, x, core], local_sem.at[0])
+    def own_rot(j):
+        return pltpu.make_async_copy(
+            rot_ref.at[:, cols(j, narrow)], gathered.at[j, y, x, core], own_sem.at[j])
+
+    def each(function, start, stop):
+        def one(j, _):
+            function(j)
+            return 0
+
+        lax.fori_loop(start, stop, one, 0)
+
     own_orb = pltpu.make_async_copy(
-        orb_ref, points.at[:, pl.ds(pl.multiple_of(z * inner, inner), inner)], local_sem.at[1])
-    own_rot.start()
+        orb_ref, points.at[:, pl.ds(pl.multiple_of(z * inner, inner), inner)], local_sem)
+    each(lambda j: own_rot(j).start(), 0, CHUNKS)
     own_orb.start()
 
     for to in (device(chip_x), device(chip_y), device(chip, 1 - core)):
@@ -123,13 +133,19 @@
     def _():
         pl.semaphore_wait(barrier, 4)
 
-    def start_early(p):
-        for d in (0, 1):
-            early(d, p).start()
-
-    def got_early(p):
-        for d in (0, 1):
-            early(d, p).wait_recv()
+    def start_early(group):
+        def one(p):
+            for d in (0, 1):
+                early(d, p).start()
+
+        each(one, group * GROUP, (group + 1) * GROUP)
+
+    def got_early(group):
+        def one(p):
+            for d in (0, 1):
+                early(d, p).wait_recv()
+
+        each(one, group * GROUP, (group + 1) * GROUP)
 
     def start_late(j):
         for d in (0, 1):
@@ -143,7 +159,7 @@
     def multiply(j):
         pair(j).wait_recv()
         where = cols(j, narrow)
-        block = gathered[:, :, :, :, where].reshape(8 * depth, narrow)
+        block = gathered[j].reshape(8 * depth, narrow)
         out_ref[:, where] = jnp.dot(
             points[...], block, preferred_element_type=jnp.float32
         ).astype(out_ref.dtype)
@@ -151,7 +167,7 @@
     line_step(0)
     start_early(0)
     start_early(1)
-    own_rot.wait()
+    each(lambda j: own_rot(j).wait(), 0, CHUNKS)
     own_orb.wait()
     got_early(0)
     start_early(2)
@@ -210,12 +226,9 @@
 
     lax.fori_loop(CHUNKS - LEFT, CHUNKS, arrived, 0)
 
-    for p in range(EARLY):
-        for d in (0, 1):
-            early(d, p).wait_send()
-
     def sent(j, _):
         for d in (0, 1):
+            early(d, j).wait_send()
             late(d, j).wait_send()
         pair(j).wait_send()
         return 0
@@ -233,25 +246,24 @@
     columns = out_ref.shape[1]
     narrow = (columns - done) // LEFT
     depth = points.shape[1]
-    block = rows // LEFT
+    block = rows // BLOCKS
     copies = []
-    for i in range(LEFT):
+    for i in range(BLOCKS):
         part = pl.ds(i * block, block)
         copies.append(pltpu.make_async_copy(
             first_ref.at[part], out_ref.at[part, pl.ds(0, done)], sems.at[i]))
-        copies[-1].start()
+        copies[-1].start(priority=i % 2)
 
     def put(i):
         start = pl.multiple_of(i * narrow, narrow)
         at = pl.multiple_of(done + i * narrow, narrow)
         return pltpu.make_async_copy(
             last.at[:, pl.ds(start, narrow)], out_ref.at[:, pl.ds(at, narrow)],
-            sems.at[LEFT + i])
+            sems.at[BLOCKS + i])
 
     def multiply(i, _):
-        at = pl.ds(pl.multiple_of(done + i * narrow, narrow), narrow)
         where = pl.ds(pl.multiple_of(i * narrow, narrow), narrow)
-        weights = gathered[:, :, :, :, at].reshape(depth, narrow)
+        weights = gathered[CHUNKS - LEFT + i].reshape(depth, narrow)
         last[:, where] = jnp.dot(
             points[...], weights, preferred_element_type=jnp.float32
         ).astype(last.dtype)
@@ -277,17 +289,17 @@
         gather_multiply,
         out_shape=(
             pltpu.VMEM((points, columns - rest), bf16),
-            pltpu.VMEM((2, 2, 2, depth, columns), bf16),
+            pltpu.VMEM((CHUNKS, 2, 2, 2, depth, columns // CHUNKS), bf16),
             pltpu.VMEM((points, 4 * inner), bf16),
         ),
         in_specs=[hbm] * 2,
         out_specs=(vmem,) * 3,
         scratch_shapes=[
-            dma((2, EARLY)), dma((2, EARLY)),
+            dma((2, CHUNKS)), dma((2, CHUNKS)),
             dma((2, CHUNKS)), dma((2, CHUNKS)),
             dma((CHUNKS,)), dma((CHUNKS,)),
             dma((2, 3)), dma((2, 3)),
-            dma((2,)),
+            dma((CHUNKS,)), dma,
         ],
         compiler_params=pltpu.CompilerParams(
             collective_id=0, has_side_effects=True, vmem_limit_bytes=16 * 2**20
@@ -308,7 +320,7 @@
         out_shape=pltpu.HBM((points, columns), bf16),
         in_specs=[vmem] * 3,
         out_specs=hbm,
-        scratch_shapes=[pltpu.VMEM((points, rest), bf16), dma((2 * LEFT,))],
+        scratch_shapes=[pltpu.VMEM((points, rest), bf16), dma((BLOCKS + LEFT,))],
         compiler_params=pltpu.CompilerParams(vmem_limit_bytes=16 * 2**20),
         cost_estimate=pl.CostEstimate(
             flops=2 * points * 8 * depth * rest,

time: 47.4 us -> 48.1 us (1.015)
  Pallas kernels: 47.2 us -> 47.9 us
    pallas_call x1, Pallas kernels: 41.3 us -> 41.9 us  [in_kernel(): pl.pallas_call(gather_multiply, out_shape=(pltpu.VMEM((points, columns -...]
where the time goes in v4:
time: 48.1 us; the launch traced here: 47.9 us
  Pallas kernels  47.9 us (100%)
    pallas_call x1, Pallas kernels, in_kernel(): pl.pallas_call(gather_multiply, out_shape=(pltpu.VMEM((points, columns -...  41.9 us
    pallas_call x1, Pallas kernels, in_kernel(): pl.pallas_call(write_rest, out_shape=pltpu.HBM((points, columns), bf16),...  5.96 us

profile of v4, /device:TPU:0, one launch (start us, length us, event | category | flops | bytes accessed | tf_op | source)
XLA Modules:
  0.0 47.9 jit_solution(9431707076489488767)
XLA Ops:
  0.0 41.9 %gather_multiply.1 = (bf16[1024,6144]{1,0:T(8,128)(2,1)S(1)}, bf16[16,2,2,2,64,512]{5,4,3,2,1,0:T(8,128)(2,1)S(1)}, bf16[1024,512]{1,0:T(8,128)(2,1)S(1)}) custom-call(bf16[1024,128]{1,0:T(8,128)(2,1)} %orb_ref.1, bf16[64,8192]{1,0:T(8,128)(2,1)} %rot_ref.1), custom_call_target="tpu_custom_call" | custom-call | flops 6442450944 | bytes 1310720 | tf_op jit(solution)/shard_map/gather_multiply/pallas_call | solution.py:288
  41.9 6.0 %write_rest.1 = bf16[1024,8192]{1,0:T(8,128)(2,1)} custom-call(bf16[1024,6144]{1,0:T(8,128)(2,1)S(1)} %get-tuple-element.8.first_ref, bf16[16,2,2,2,64,512]{5,4,3,2,1,0:T(8,128)(2,1)S(1)} %get-tuple-element.9.gathered, bf16[1024,512]{1,0:T(8,128)(2,1)S(1)} %get-tuple-element.10.points), custom_call_target="tpu_custom_call" | custom-call | flops 2147483648 | bytes 16777216 | tf_op jit(solution)/shard_map/write_rest/pallas_call | solution.py:318

commit v5 on v2

--- a/solution.py
+++ b/solution.py
@@ -10,7 +10,8 @@
 CHUNKS = 16
 EARLY = 4
 AHEAD = 5
-LEFT = 4
+LEFT = 5
+BLOCKS = 4
 
 
 def gather_multiply(
@@ -99,8 +100,6 @@
     own_rot = pltpu.make_async_copy(rot_ref, gathered.at[y, x, core], local_sem.at[0])
     own_orb = pltpu.make_async_copy(
         orb_ref, points.at[:, pl.ds(pl.multiple_of(z * inner, inner), inner)], local_sem.at[1])
-    own_rot.start()
-    own_orb.start()
 
     for to in (device(chip_x), device(chip_y), device(chip, 1 - core)):
         greet(to)
@@ -113,6 +112,8 @@
     def _():
         greet(device(chip, core, z + 1))
 
+    own_rot.start()
+    own_orb.start()
     middle = (z > 0) & (z < nz - 1)
 
     @pl.when(middle)
@@ -148,8 +149,8 @@
             points[...], block, preferred_element_type=jnp.float32
         ).astype(out_ref.dtype)
 
+    start_early(0)
     line_step(0)
-    start_early(0)
     start_early(1)
     own_rot.wait()
     own_orb.wait()
@@ -233,9 +234,9 @@
     columns = out_ref.shape[1]
     narrow = (columns - done) // LEFT
     depth = points.shape[1]
-    block = rows // LEFT
+    block = rows // BLOCKS
     copies = []
-    for i in range(LEFT):
+    for i in range(BLOCKS):
         part = pl.ds(i * block, block)
         copies.append(pltpu.make_async_copy(
             first_ref.at[part], out_ref.at[part, pl.ds(0, done)], sems.at[i]))
@@ -246,7 +247,7 @@
         at = pl.multiple_of(done + i * narrow, narrow)
         return pltpu.make_async_copy(
             last.at[:, pl.ds(start, narrow)], out_ref.at[:, pl.ds(at, narrow)],
-            sems.at[LEFT + i])
+            sems.at[BLOCKS + i])
 
     def multiply(i, _):
         at = pl.ds(pl.multiple_of(done + i * narrow, narrow), narrow)
@@ -308,7 +309,7 @@
         out_shape=pltpu.HBM((points, columns), bf16),
         in_specs=[vmem] * 3,
         out_specs=hbm,
-        scratch_shapes=[pltpu.VMEM((points, rest), bf16), dma((2 * LEFT,))],
+        scratch_shapes=[pltpu.VMEM((points, rest), bf16), dma((BLOCKS + LEFT,))],
         compiler_params=pltpu.CompilerParams(vmem_limit_bytes=16 * 2**20),
         cost_estimate=pl.CostEstimate(
             flops=2 * points * 8 * depth * rest,

time: 47.4 us -> 47.4 us (level)
  no operation moved by 1% of the time
where the time goes in v5:
time: 47.4 us; the launch traced here: 47.2 us
  Pallas kernels  47.2 us (100%)
    pallas_call x1, Pallas kernels, in_kernel(): pl.pallas_call(gather_multiply, out_shape=(pltpu.VMEM((points, columns -...  41.3 us
    pallas_call x1, Pallas kernels, in_kernel(): pl.pallas_call(write_rest, out_shape=pltpu.HBM((points, columns), bf16),...  5.95 us

profile of v5, /device:TPU:0, one launch (start us, length us, event | category | flops | bytes accessed | tf_op | source)
XLA Modules:
  0.0 47.2 jit_solution(7645338464977844351)
XLA Ops:
  0.0 41.3 %gather_multiply.1 = (bf16[1024,5632]{1,0:T(8,128)(2,1)S(1)}, bf16[2,2,2,64,8192]{4,3,2,1,0:T(8,128)(2,1)S(1)}, bf16[1024,512]{1,0:T(8,128)(2,1)S(1)}) custom-call(bf16[1024,128]{1,0:T(8,128)(2,1)} %orb_ref.1, bf16[64,8192]{1,0:T(8,128)(2,1)} %rot_ref.1), custom_call_target="tpu_custom_call" | custom-call | flops 5905580032 | bytes 1310720 | tf_op jit(solution)/shard_map/gather_multiply/pallas_call | solution.py:277
  41.3 5.9 %write_rest.1 = bf16[1024,8192]{1,0:T(8,128)(2,1)} custom-call(bf16[1024,5632]{1,0:T(8,128)(2,1)S(1)} %get-tuple-element.8.first_ref, bf16[2,2,2,64,8192]{4,3,2,1,0:T(8,128)(2,1)S(1)} %get-tuple-element.9.gathered, bf16[1024,512]{1,0:T(8,128)(2,1)S(1)} %get-tuple-element.10.points), custom_call_target="tpu_custom_call" | custom-call | flops 2684354560 | bytes 16777216 | tf_op jit(solution)/shard_map/write_rest/pallas_call | solution.py:307

commit v6 on v5

--- a/solution.py
+++ b/solution.py
@@ -9,7 +9,7 @@
 
 CHUNKS = 16
 EARLY = 4
-AHEAD = 5
+AHEAD = 3
 LEFT = 5
 BLOCKS = 4
 

time: 47.4 us -> 48.9 us (1.032)
  Pallas kernels: 47.2 us -> 48.7 us
    pallas_call x1, Pallas kernels: 41.3 us -> 42.8 us  [in_kernel(): pl.pallas_call(gather_multiply, out_shape=(pltpu.VMEM((points, columns -...]
where the time goes in v6:
time: 48.9 us; the launch traced here: 48.7 us
  Pallas kernels  48.7 us (100%)
    pallas_call x1, Pallas kernels, in_kernel(): pl.pallas_call(gather_multiply, out_shape=(pltpu.VMEM((points, columns -...  42.8 us
    pallas_call x1, Pallas kernels, in_kernel(): pl.pallas_call(write_rest, out_shape=pltpu.HBM((points, columns), bf16),...  5.95 us

profile of v6, /device:TPU:0, one launch (start us, length us, event | category | flops | bytes accessed | tf_op | source)
XLA Modules:
  0.0 48.7 jit_solution(2190901885170586155)
XLA Ops:
  0.0 42.8 %gather_multiply.1 = (bf16[1024,5632]{1,0:T(8,128)(2,1)S(1)}, bf16[2,2,2,64,8192]{4,3,2,1,0:T(8,128)(2,1)S(1)}, bf16[1024,512]{1,0:T(8,128)(2,1)S(1)}) custom-call(bf16[1024,128]{1,0:T(8,128)(2,1)} %orb_ref.1, bf16[64,8192]{1,0:T(8,128)(2,1)} %rot_ref.1), custom_call_target="tpu_custom_call" | custom-call | flops 5905580032 | bytes 1310720 | tf_op jit(solution)/shard_map/gather_multiply/pallas_call | solution.py:277
  42.8 5.9 %write_rest.1 = bf16[1024,8192]{1,0:T(8,128)(2,1)} custom-call(bf16[1024,5632]{1,0:T(8,128)(2,1)S(1)} %get-tuple-element.8.first_ref, bf16[2,2,2,64,8192]{4,3,2,1,0:T(8,128)(2,1)S(1)} %get-tuple-element.9.gathered, bf16[1024,512]{1,0:T(8,128)(2,1)S(1)} %get-tuple-element.10.points), custom_call_target="tpu_custom_call" | custom-call | flops 2684354560 | bytes 16777216 | tf_op jit(solution)/shard_map/write_rest/pallas_call | solution.py:307
